TPU v7x, 32 devices: a whole 2x2x4 slice. The times are simulated.
32 devices in a mesh: query: 2 (over x), corpus: 16 (over z, y, core).
Axes of the slice: x: 2, y: 2, z: 4, core: 2. Of those that a mesh axis runs over, the one named last changes fastest.
Arguments:
- clean_feats: bfloat16 [2, 2, 512, 320], P('query', None, 'corpus'), may hold values from -6 to 6
- noise_draw: bfloat16 [2, 2, 512, 320], P('query', None, 'corpus'), may hold values from -6 to 6
- timesteps: int32 [2, 2], P('query'), may hold values from 0 to 999
- weight_in: bfloat16 [2, 320, 320], P(None, None, 'corpus'), may hold values from -0.3125 to 0.3125
- weight_ffin: bfloat16 [2, 320, 2560], P(None, None, 'corpus'), may hold values from -0.3125 to 0.3125
- weight_ffout: bfloat16 [2, 1280, 320], P(None, None, 'corpus'), may hold values from -0.15625 to 0.15625
- weight_out: bfloat16 [2, 320, 320], P(None, None, 'corpus'), may hold values from -0.3125 to 0.3125
- norm_gain: float32 [2, 320], replicated, may hold values from 0.5 to 1.5
- norm_bias: float32 [2, 320], replicated, may hold values from -3 to 3
- sketch_cin: bfloat16 [2, 3, 320, 16], replicated, may hold values from -0.3125 to 0.3125
- sketch_fin: bfloat16 [2, 1280, 16], replicated, may hold values from -0.15625 to 0.15625
- sketch_cout: bfloat16 [2, 3, 320, 16], replicated, may hold values from -0.3125 to 0.3125
- sketch_fout: bfloat16 [2, 2560, 16], replicated, may hold values from -0.125 to 0.125
- precond: float32 [8, 256, 256], P('query'), as said below
- store_grads: bfloat16 [8192, 2048], P(('query', 'corpus')), may hold values from -6 to 6
- store_scale: float32 [8192], P(('query', 'corpus')), may hold values from 0.002 to 0.03
Outputs:
- scores: float32 [2, 8192], P(None, ('query', 'corpus'))
Inputs may be any that keep to these rules, and one draw needn't show every extreme that they name: `precond`: each layer's matrix is symmetric with a diagonal between 1 and 2.
All inputs are finite; a program needn't handle non-finite values.
Results may differ from a plain program's by a relative error of at most 0.0085.
Values may be sent and summed in bfloat16 or wider, within the bound.
A program may use at most 64 MiB of HBM per device.

v0:
```python
import math

import jax
import jax.numpy as jnp
from jax import lax
from jax.sharding import PartitionSpec as P

plan_len = 1000


def noise_levels(timesteps):
    steps = jnp.arange(plan_len, dtype=jnp.float32)
    rooted = math.sqrt(0.00085) + (math.sqrt(0.012) - math.sqrt(0.00085)) * steps / (plan_len - 1)
    cumulative = jnp.exp(jnp.cumsum(jnp.log1p(-rooted * rooted)))
    matches = timesteps[..., None] == jnp.arange(plan_len, dtype=jnp.int32)
    picked = jnp.sum(jnp.where(matches, cumulative, jnp.zeros_like(cumulative)), axis=-1)
    return (jnp.sqrt(picked), jnp.sqrt(1.0 - picked))


def gelu_parts(gate):
    cumul = 0.5 * (1.0 + jax.scipy.special.erf(gate / math.sqrt(2.0)))
    density = jnp.exp(-0.5 * gate * gate) / math.sqrt(2.0 * math.pi)
    return (gate * cumul, cumul + gate * density)


def contract_back(delta, weight):
    return lax.dot_general(
        delta, weight, (((1,), (1,)), ((), ())), preferred_element_type=jnp.float32
    )


def block_forward(residual_stream, weights, scale_gain, shift_bias):
    weight_in, weight_ffin, weight_ffout, weight_out = weights
    hidden = weight_ffout.shape[0]
    residual_reduced = residual_stream.astype(jnp.bfloat16)
    inner = jnp.dot(residual_reduced, weight_in, preferred_element_type=jnp.float32)
    centred_input = inner - jnp.mean(inner, axis=-1, keepdims=True)
    inverse_deviation = lax.rsqrt(
        jnp.mean(centred_input * centred_input, axis=-1, keepdims=True) + 1e-05
    )
    standardized_input = centred_input * inverse_deviation
    normalized_input = (standardized_input * scale_gain + shift_bias).astype(jnp.bfloat16)
    projected = jnp.dot(normalized_input, weight_ffin, preferred_element_type=jnp.float32)
    value_output = projected[:, :hidden]
    gate = projected[:, hidden:]
    gelu_result, gelu_derivative = gelu_parts(gate)
    mixed_hidden = (value_output * gelu_result).astype(jnp.bfloat16)
    inner_two = inner + jnp.dot(mixed_hidden, weight_ffout, preferred_element_type=jnp.float32)
    inner_reduced = inner_two.astype(jnp.bfloat16)
    residual_stream = residual_stream + jnp.dot(
        inner_reduced, weight_out, preferred_element_type=jnp.float32
    )
    return (
        residual_stream,
        (
            residual_reduced,
            standardized_input,
            inverse_deviation,
            normalized_input,
            value_output,
            gelu_result,
            gelu_derivative,
            mixed_hidden,
            inner_reduced,
        ),
    )


def block_backward(dstream, saved_activations, weights, scale_gain):
    weight_in, weight_ffin, weight_ffout, weight_out = weights
    (
        residual_reduced,
        standardized_input,
        inverse_deviation,
        normalized_input,
        value_output,
        gelu_result,
        gelu_derivative,
        mixed_hidden,
        inner_reduced,
    ) = saved_activations
    dout_low = dstream.astype(jnp.bfloat16)
    second_inner_gradient = contract_back(dout_low, weight_out)
    dtwo_low = second_inner_gradient.astype(jnp.bfloat16)
    dmixed = contract_back(dtwo_low, weight_ffout)
    dproj_low = jnp.concatenate(
        [dmixed * gelu_result, dmixed * value_output * gelu_derivative], axis=-1
    ).astype(jnp.bfloat16)
    dnormed = contract_back(dproj_low, weight_ffin)
    scaled_hidden = dnormed * scale_gain
    inner_gradient = second_inner_gradient + inverse_deviation * (
        scaled_hidden
        - jnp.mean(scaled_hidden, axis=-1, keepdims=True)
        - standardized_input * jnp.mean(scaled_hidden * standardized_input, axis=-1, keepdims=True)
    )
    dinner_low = inner_gradient.astype(jnp.bfloat16)
    dstream = dstream + contract_back(dinner_low, weight_in)
    records = [
        (residual_reduced, dinner_low),
        (normalized_input, dproj_low),
        (mixed_hidden, dtwo_low),
        (inner_reduced, dout_low),
    ]
    return (dstream, records)


def project_layer(inputs, deltas, sketch_in, sketch_out, samples):
    left = jnp.dot(inputs, sketch_in, preferred_element_type=jnp.float32)
    right = jnp.dot(deltas, sketch_out, preferred_element_type=jnp.float32)
    left = left.reshape(samples, -1, left.shape[-1])
    right = right.reshape(samples, -1, right.shape[-1])
    outer = jnp.einsum("srk,srj->skj", left, right, precision=lax.Precision.HIGHEST)
    return outer.reshape(samples, -1)


def sketches_of(block, sketch_cin, sketch_fin, sketch_cout, sketch_fout):
    return [
        (sketch_cin[block, 0], sketch_cout[block, 0]),
        (sketch_cin[block, 1], sketch_fout[block]),
        (sketch_fin[block], sketch_cout[block, 1]),
        (sketch_cin[block, 2], sketch_cout[block, 2]),
    ]


def on_device(
    clean_feats,
    noise_draw,
    timesteps,
    weight_in,
    weight_ffin,
    weight_ffout,
    weight_out,
    norm_gain,
    norm_bias,
    sketch_cin,
    sketch_fin,
    sketch_cout,
    sketch_fout,
    precond,
    store_grads,
    store_scale,
):
    samples = clean_feats.shape[0]
    positions = clean_feats.shape[2] * lax.axis_size("corpus")
    loss_scale = 1.0 / math.sqrt(clean_feats.shape[1] * positions)
    blocks = weight_in.shape[0]
    signal, spread = noise_levels(timesteps)
    noise_rows = noise_draw.astype(jnp.float32)
    residual_stream = (
        signal[:, :, None, None] * clean_feats.astype(jnp.float32)
        + spread[:, :, None, None] * noise_rows
    )
    residual_stream = residual_stream.reshape(-1, residual_stream.shape[-1])
    noise_rows = noise_rows.reshape(-1, noise_rows.shape[-1])
    gathered = (
        lax.all_gather(weight_in, "corpus", axis=2, tiled=True),
        lax.all_gather(weight_ffin, "corpus", axis=2, tiled=True),
        lax.all_gather(weight_ffout, "corpus", axis=2, tiled=True),
        lax.all_gather(weight_out, "corpus", axis=2, tiled=True),
    )

    def fetch_forward(block):
        return tuple((member[block] for member in gathered))

    def fetch_backward(block):
        return tuple((member[block] for member in gathered))

    saved_all = []
    for block in range(blocks):
        residual_stream, saved_activations = block_forward(
            residual_stream, fetch_forward(block), norm_gain[block], norm_bias[block]
        )
        saved_all.append(saved_activations)
    dstream = (residual_stream - noise_rows) * loss_scale
    layers = [None] * (4 * blocks)
    for block in reversed(range(blocks)):
        dstream, records = block_backward(
            dstream, saved_all[block], fetch_backward(block), norm_gain[block]
        )
        pairs = sketches_of(block, sketch_cin, sketch_fin, sketch_cout, sketch_fout)
        for index in range(4):
            layers[4 * block + index] = project_layer(
                records[index][0], records[index][1], pairs[index][0], pairs[index][1], samples
            )
    partial_grads = jnp.stack(layers, axis=1)
    totals = lax.psum(partial_grads, "corpus")
    routed = lax.all_to_all(totals, "query", split_axis=1, concat_axis=0, tiled=True)
    owned = jnp.einsum("qlk,lkj->qlj", routed, precond, precision=lax.Precision.HIGHEST).astype(
        jnp.bfloat16
    )
    preconditioned = lax.all_gather(owned, "query", axis=1, tiled=True)
    flat = preconditioned.reshape(preconditioned.shape[0], -1)
    raw = lax.dot_general(
        flat, store_grads, (((1,), (1,)), ((), ())), preferred_element_type=jnp.float32
    )
    return raw * store_scale[None, :]


def solution(mesh):
    placed = (
        P("query", None, "corpus", None),
        P("query", None, "corpus", None),
        P("query", None),
        P(None, None, "corpus"),
        P(None, None, "corpus"),
        P(None, None, "corpus"),
        P(None, None, "corpus"),
        P(),
        P(),
        P(),
        P(),
        P(),
        P(),
        P("query", None, None),
        P(("query", "corpus"), None),
        P(("query", "corpus")),
    )
    return jax.shard_map(
        on_device,
        mesh=mesh,
        in_specs=placed,
        out_specs=P(None, ("query", "corpus")),
        check_vma=False,
    )
```

profile of v0, /device:TPU:0, one launch (start us, length us, event | category | flops | bytes accessed | tf_op | source)
XLA Modules:
  0.0 166.5 jit_solution(25093315047385760)
XLA Ops:
  6.5 0.7 all-gather.5.cloned.1.call-update
  7.3 0.7 all-gather.3.cloned.1.call-update
  8.0 0.3 reduce-window.9
  8.4 24.9 %all_gather.15 = bf16[2,320,320]{1,0,2:T(2,128)(2,1)S(1)} all-gather(bf16[2,320,20]{1,0,2:T(2,128)(2,1)} %param.19), channel_id=1, replica_groups=mesh['query'=2,'corpus'=16] {'corpus'}, dimensions={2}, use_global_device_ids=true | all-gather | bytes 435200 | tf_op jit(solution)/shard_map/all_gather | solution.py:156
  33.3 0.7 fusion.105
  34.0 0.9 copy.52
  34.9 20.2 %all_gather.18 = bf16[2,320,320]{1,0,2:T(2,128)(2,1)S(1)} all-gather(bf16[2,320,20]{1,0,2:T(2,128)(2,1)S(1)} %copy-done.12), channel_id=1, replica_groups=mesh['query'=2,'corpus'=16] {'corpus'}, dimensions={2}, use_global_device_ids=true | all-gather | bytes 435200 | tf_op jit(solution)/shard_map/all_gather | solution.py:159
  55.1 0.7 fusion.104
  55.8 0.9 copy.54
  56.7 0.9 copy.55
  57.6 0.9 copy.57
  58.6 0.6 slice_reduce_fusion.1
  59.3 0.2 fusion.93
  59.5 0.7 fusion.102
  60.3 0.3 fusion.107
  60.5 0.2 multiply_reduce_fusion.3
  60.7 0.8 fusion.79
  61.7 0.6 copy-done.4
  62.3 0.8 fusion.76
  63.2 5.7 %fusion.103 = (bf16[1,1280,320]{1,0,2:T(2,128)(2,1)}, bf16[1,1280,320]{1,0,2:T(2,128)(2,1)S(1)}) fusion(bf16[2,1280,320]{1,0,2:T(2,128)(2,1)} %all-gather.5.cloned.1.call-done), kind=kLoop, calls=%fused_computation.164 | loop fusion | bytes 3276800 | tf_op jit(solution)/shard_map/slice | solution.py:163
  68.8 34.3 %all-gather.3.cloned.1.call-done = bf16[2,320,2560]{1,2,0:T(8,128)(2,1)} async-done(((bf16[2,320,160]{1,2,0:T(8,128)(2,1)}), bf16[2,320,2560]{1,2,0:T(8,128)(2,1)}) %all-gather.3.cloned.1.call-update) | async-done | bytes 3276816 | tf_op jit(solution)/shard_map/all_gather | solution.py:157
  103.1 2.5 %fusion.1 = f32[64,2560]{1,0:T(8,128)S(1)} fusion(bf16[64,320]{1,0:T(8,128)(2,1)} %copy-done.4, bf16[2,320,2560]{1,2,0:T(8,128)(2,1)} %all-gather.3.cloned.1.call-done), kind=kOutput, calls=%fused_computation.3 | convolution fusion | flops 104857600 | bytes 2670592 | tf_op jit(solution)/shard_map/dot_general | solution.py:43
  105.7 0.4 fusion.8
  106.1 0.1 fusion.73
  106.2 0.2 convolution_add_fusion.4
  106.4 0.3 fusion.108
  106.7 0.2 multiply_reduce_fusion.2
  107.0 0.7 fusion.3
  107.8 0.3 copy-done.2
  108.1 0.4 fusion.9
  108.5 0.2 fusion.7
  108.6 0.2 fusion.26
  108.8 0.3 multiply_convert_fusion.1
  109.2 0.5 fusion.101
  109.8 0.2 fusion.10
  110.1 0.2 fusion.32
  110.3 0.3 multiply_convert_fusion
  110.6 0.1 fusion.50
  110.7 0.1 fusion.71
  110.9 0.1 fusion.59
  111.0 0.1 fusion.68
  111.1 0.1 fusion.66
  111.3 0.1 fusion.46
  111.4 0.2 fusion.44
  111.6 0.2 fusion.53
  111.8 0.1 fusion.63
  111.9 0.1 fusion.56
  112.0 0.2 fusion.38
  112.2 0.2 fusion.37
  112.5 0.5 fusion.100
  113.0 0.2 fusion.43
  113.3 0.1 fusion.109
  113.5 0.1 fusion.110
  113.7 0.1 fusion.111
  113.9 0.1 fusion.112
  114.2 0.1 fusion.113
  114.4 0.1 fusion.114
  114.6 0.1 fusion.115
  114.8 0.1 fusion.116
  115.1 32.2 %psum.7 = f32[1,8,256]{2,0,1:T(1,128)S(1)} all-reduce(f32[1,8,256]{2,0,1:T(1,128)S(1)} %constant_dynamic-update-slice_fusion), channel_id=1, replica_groups=mesh['query'=2,'corpus'=16] {'corpus'}, use_global_device_ids=true, to_apply=%region_11.12 | all-reduce | flops 2048 | bytes 16384 | tf_op jit(solution)/shard_map/psum | solution.py:186
  147.4 6.3 %all_to_all.12 = f32[1,8,256]{2,0,1:T(1,128)S(1)} all-to-all(f32[1,8,256]{2,0,1:T(1,128)S(1)} %psum.7), channel_id=1, replica_groups=mesh['query'=2,'corpus'=16] {'query'}, dimensions={1} | all-to-all | bytes 16384 | tf_op jit(solution)/shard_map/all_to_all | solution.py:187
  153.8 0.6 fusion.11
  154.4 4.3 %all_gather.19 = bf16[2,8,256]{2,0,1:T(2,128)(2,1)S(1)} all-gather(bf16[2,4,256]{2,0,1:T(2,128)(2,1)S(1)} %fusion.11), channel_id=1, replica_groups=mesh['query'=2,'corpus'=16] {'query'}, dimensions={1}, use_global_device_ids=true | all-gather | bytes 12288 | tf_op jit(solution)/shard_map/all_gather | solution.py:191
  158.7 1.0 convolution_multiply_fusion
  (86 shorter events, 1.8 us)
Async XLA Ops:
  6.5 147.2 %copy-start = (f32[4,256,256]{2,1,0:T(8,128)S(1)}, f32[4,256,256]{2,1,0:T(8,128)}, u32[]{:S(2)}) copy-start(f32[4,256,256]{2,1,0:T(8,128)} %param.29) | copy-start | bytes 3145732
  6.5 28.4 %copy-start.12 = (bf16[2,320,20]{1,0,2:T(2,128)(2,1)S(1)}, bf16[2,320,20]{1,0,2:T(2,128)(2,1)}, u32[]{:S(2)}) copy-start(bf16[2,320,20]{1,0,2:T(2,128)(2,1)} %param.22) | copy-start | bytes 76804
  6.5 56.6 %all-gather.5.cloned.1.call-start = ((), (), s32[]{:S(2)}) async-start(), calls=%async_computation.2 | async-start | bytes 1740800 | tf_op jit(solution)/shard_map/all_gather | solution.py:158
  7.3 95.8 %all-gather.3.cloned.1.call-start = ((), (), s32[]{:S(2)}) async-start(), calls=%async_computation.1 | async-start | bytes 4177920 | tf_op jit(solution)/shard_map/all_gather | solution.py:157
  55.1 3.5 %copy-start.16 = (f32[2,320]{1,0:T(2,128)S(1)}, f32[2,320]{1,0:T(2,128)}, u32[]{:S(2)}) copy-start(f32[2,320]{1,0:T(2,128)} %param.24) | copy-start | bytes 7684
  55.1 4.1 %copy-start.17 = (f32[2,320]{1,0:T(2,128)S(1)}, f32[2,320]{1,0:T(2,128)}, u32[]{:S(2)}) copy-start(f32[2,320]{1,0:T(2,128)} %param.23) | copy-start | bytes 7684
  55.1 4.2 %copy-start.21 = (s32[1,2]{1,0:T(1,128)S(1)}, s32[1,2]{1,0:T(1,128)}, u32[]{:S(2)}) copy-start(s32[1,2]{1,0:T(1,128)} %param.18) | copy-start | bytes 28
  55.1 4.4 %copy-start.6 = (bf16[1,2,32,320]{3,2,1,0:T(8,128)(2,1)S(1)}, bf16[1,2,32,320]{3,2,1,0:T(8,128)(2,1)}, u32[]{:S(2)}) copy-start(bf16[1,2,32,320]{3,2,1,0:T(8,128)(2,1)} %param.17) | copy-start | bytes 122884
  55.1 4.4 %copy-start.11 = (bf16[1,2,32,320]{3,2,1,0:T(8,128)(2,1)S(1)}, bf16[1,2,32,320]{3,2,1,0:T(8,128)(2,1)}, u32[]{:S(2)}) copy-start(bf16[1,2,32,320]{3,2,1,0:T(8,128)(2,1)} %param.16) | copy-start | bytes 122884
  60.5 8.3 %copy-start.14 = (f32[64]{0:T(128)}, f32[64]{0:T(128)S(1)}, u32[]{:S(2)}) copy-start(f32[64]{0:T(128)S(1)} %broadcast_multiply_fusion.5) | copy-start | bytes 772
  60.7 2.4 %copy-start.18 = (f32[64]{0:T(128)}, f32[64]{0:T(128)S(1)}, u32[]{:S(2)}) copy-start(f32[64]{0:T(128)S(1)} %add_rsqrt_fusion.1) | copy-start | bytes 772
  61.7 0.6 copy-start.4
  103.1 2.9 %copy-start.10 = (bf16[2,3,320,16]{2,3,1,0:T(8,128)(2,1)S(1)}, bf16[2,3,320,16]{2,3,1,0:T(8,128)(2,1)}, u32[]{:S(2)}) copy-start(bf16[2,3,320,16]{2,3,1,0:T(8,128)(2,1)} %param.25) | copy-start | bytes 184324
  103.1 3.1 %copy-start.5 = (f32[1,2,32,320]{3,2,1,0:T(8,128)S(1)}, f32[1,2,32,320]{3,2,1,0:T(8,128)}, u32[]{:S(2)}) copy-start(f32[1,2,32,320]{3,2,1,0:T(8,128)} %get-tuple-element.14) | copy-start | bytes 245764
  103.1 3.9 %copy-start.1 = (bf16[2,320,2560]{1,2,0:T(8,128)(2,1)S(1)}, bf16[2,320,2560]{1,2,0:T(8,128)(2,1)}, u32[]{:S(2)}) copy-start(bf16[2,320,2560]{1,2,0:T(8,128)(2,1)} %all-gather.3.cloned.1.call-done) | copy-start | bytes 9830404
  105.6 1.3 copy-start.13
  106.6 1.4 copy-start.2
  107.0 1.5 copy-start.7
  109.7 0.9 copy-start.9
  109.7 1.6 copy-start.8
  110.1 2.0 %copy-start.22 = (bf16[2,2560,16]{1,2,0:T(8,128)(2,1)S(1)}, bf16[2,2560,16]{1,2,0:T(8,128)(2,1)}, u32[]{:S(2)}) copy-start(bf16[2,2560,16]{1,2,0:T(8,128)(2,1)} %param.28) | copy-start | bytes 491524
  110.3 2.2 %copy-start.15 = (f32[64]{0:T(128)S(1)}, f32[64]{0:T(128)}, u32[]{:S(2)}) copy-start(f32[64]{0:T(128)} %copy-done.14) | copy-start | bytes 772
  110.3 2.2 %copy-start.19 = (f32[64]{0:T(128)S(1)}, f32[64]{0:T(128)}, u32[]{:S(2)}) copy-start(f32[64]{0:T(128)} %copy-done.18) | copy-start | bytes 772
  112.4 46.3 %copy-start.3 = (bf16[256,2048]{1,0:T(8,128)(2,1)S(1)}, bf16[256,2048]{1,0:T(8,128)(2,1)}, u32[]{:S(2)}) copy-start(bf16[256,2048]{1,0:T(8,128)(2,1)} %param.30) | copy-start | bytes 3145732
  112.5 46.3 %copy-start.20 = (f32[256]{0:T(256)S(1)}, f32[256]{0:T(256)}, u32[]{:S(2)}) copy-start(f32[256]{0:T(256)} %param.31) | copy-start | bytes 3076
Sparse Core Ops, SparseCore 0:
  9.5 43.6 all-gather.4
  55.5 47.5 all-gather.2
where the time goes:
time: 167 us
  blocking collectives  88 us (53%)
  waiting for transfers between devices  35.7 us (21%)
  between operations  13.9 us (8%)
  matrix products  13.5 us (8%)
  local copies, waits for them, and re-layouts  13.2 us (8%)
  other arithmetic  2.2 us (1%)
    all_gather x1, waiting for transfers between devices, on_device(): lax.all_gather(weight_ffin, 'corpus', axis=2, tiled=True)  34.3 us
    psum x1, blocking collectives, on_device(): totals = lax.psum(partial_grads, 'corpus')  32.2 us
    all_gather x1, blocking collectives, on_device(): lax.all_gather(weight_in, 'corpus', axis=2, tiled=True)  24.9 us
    all_gather x1, blocking collectives, on_device(): lax.all_gather(weight_out, 'corpus', axis=2, tiled=True)  20.2 us
    slice x3, local copies, waits for them, and re-layouts, fetch_forward(): return tuple((member[block] for member in gathered))  7.04 us
    all_to_all x1, blocking collectives, on_device(): lax.all_to_all(totals, 'query', split_axis=1, concat_axis=0, tiled=True)  6.35 us
    unnamed x57, local copies, waits for them, and re-layouts  4.61 us
    all_gather x1, blocking collectives, on_device(): preconditioned = lax.all_gather(owned, 'query', axis=1, tiled=True)  4.33 us
  transfers between devices with their start and end apart: 2, of which 1 were waited for; matrix products, arithmetic and copies ran while one was open for 9% of the time, Pallas kernels for 0%

commit v1 on v0

--- a/solution.py
+++ b/solution.py
@@ -11,9 +11,9 @@
 def noise_levels(timesteps):
     steps = jnp.arange(plan_len, dtype=jnp.float32)
     rooted = math.sqrt(0.00085) + (math.sqrt(0.012) - math.sqrt(0.00085)) * steps / (plan_len - 1)
-    cumulative = jnp.exp(jnp.cumsum(jnp.log1p(-rooted * rooted)))
-    matches = timesteps[..., None] == jnp.arange(plan_len, dtype=jnp.int32)
-    picked = jnp.sum(jnp.where(matches, cumulative, jnp.zeros_like(cumulative)), axis=-1)
+    terms = jnp.log1p(-rooted * rooted)
+    reached = jnp.arange(plan_len, dtype=jnp.int32) <= timesteps[..., None]
+    picked = jnp.exp(jnp.sum(jnp.where(reached, terms, jnp.zeros_like(terms)), axis=-1))
     return (jnp.sqrt(picked), jnp.sqrt(1.0 - picked))
 
 

time: 167 us -> 168 us (level)
  waiting for transfers between devices: 35.7 us -> 37.9 us
    all_gather x1, waiting for transfers between devices: 34.3 us -> 36.5 us  [on_device(): lax.all_gather(weight_ffin, 'corpus', axis=2, tiled=True)]
where the time goes in v1:
time: 168 us
  blocking collectives  87.6 us (52%)
  waiting for transfers between devices  37.9 us (23%)
  between operations  13.9 us (8%)
  matrix products  13.5 us (8%)
  local copies, waits for them, and re-layouts  13 us (8%)
  other arithmetic  1.84 us (1%)
    all_gather x1, waiting for transfers between devices, on_device(): lax.all_gather(weight_ffin, 'corpus', axis=2, tiled=True)  36.5 us
    psum x1, blocking collectives, on_device(): totals = lax.psum(partial_grads, 'corpus')  32.2 us
    all_gather x1, blocking collectives, on_device(): lax.all_gather(weight_in, 'corpus', axis=2, tiled=True)  25 us
    all_gather x1, blocking collectives, on_device(): lax.all_gather(weight_out, 'corpus', axis=2, tiled=True)  19.7 us
    slice x3, local copies, waits for them, and re-layouts, fetch_forward(): return tuple((member[block] for member in gathered))  7.04 us
    all_to_all x1, blocking collectives, on_device(): lax.all_to_all(totals, 'query', split_axis=1, concat_axis=0, tiled=True)  6.35 us
    unnamed x57, local copies, waits for them, and re-layouts  4.61 us
    all_gather x1, blocking collectives, on_device(): preconditioned = lax.all_gather(owned, 'query', axis=1, tiled=True)  4.33 us
  transfers between devices with their start and end apart: 2, of which 1 were waited for; matrix products, arithmetic and copies ran while one was open for 9% of the time, Pallas kernels for 0%

profile of v1, /device:TPU:0, one launch (start us, length us, event | category | flops | bytes accessed | tf_op | source)
XLA Modules:
  0.0 167.8 jit_solution(465755251760985908)
XLA Ops:
  6.5 0.7 all-gather.5.cloned.1.call-update
  7.3 0.7 all-gather.3.cloned.1.call-update
  8.0 25.0 %all_gather.15 = bf16[2,320,320]{1,0,2:T(2,128)(2,1)S(1)} all-gather(bf16[2,320,20]{1,0,2:T(2,128)(2,1)} %param.19), channel_id=1, replica_groups=mesh['query'=2,'corpus'=16] {'corpus'}, dimensions={2}, use_global_device_ids=true | all-gather | bytes 435200 | tf_op jit(solution)/shard_map/all_gather | solution.py:156
  33.0 0.7 fusion.105
  33.7 0.9 copy.52
  34.6 19.7 %all_gather.18 = bf16[2,320,320]{1,0,2:T(2,128)(2,1)S(1)} all-gather(bf16[2,320,20]{1,0,2:T(2,128)(2,1)S(1)} %copy-done.12), channel_id=1, replica_groups=mesh['query'=2,'corpus'=16] {'corpus'}, dimensions={2}, use_global_device_ids=true | all-gather | bytes 435200 | tf_op jit(solution)/shard_map/all_gather | solution.py:159
  54.3 0.7 fusion.104
  55.0 0.9 copy.54
  55.9 0.9 copy.55
  56.8 0.9 copy.57
  57.7 0.6 slice_reduce_fusion
  58.3 0.2 fusion.93
  58.6 0.7 fusion.102
  59.3 0.3 fusion.106
  59.6 0.2 multiply_reduce_fusion.3
  59.8 0.8 fusion.79
  60.7 0.6 copy-done.4
  61.3 0.8 fusion.76
  62.2 5.7 %fusion.103 = (bf16[1,1280,320]{1,0,2:T(2,128)(2,1)}, bf16[1,1280,320]{1,0,2:T(2,128)(2,1)S(1)}) fusion(bf16[2,1280,320]{1,0,2:T(2,128)(2,1)} %all-gather.5.cloned.1.call-done), kind=kLoop, calls=%fused_computation.161 | loop fusion | bytes 3276800 | tf_op jit(solution)/shard_map/slice | solution.py:163
  67.9 36.5 %all-gather.3.cloned.1.call-done = bf16[2,320,2560]{1,2,0:T(8,128)(2,1)} async-done(((bf16[2,320,160]{1,2,0:T(8,128)(2,1)}), bf16[2,320,2560]{1,2,0:T(8,128)(2,1)}) %all-gather.3.cloned.1.call-update) | async-done | bytes 3276816 | tf_op jit(solution)/shard_map/all_gather | solution.py:157
  104.3 2.5 %fusion.1 = f32[64,2560]{1,0:T(8,128)S(1)} fusion(bf16[64,320]{1,0:T(8,128)(2,1)} %copy-done.4, bf16[2,320,2560]{1,2,0:T(8,128)(2,1)} %all-gather.3.cloned.1.call-done), kind=kOutput, calls=%fused_computation.3 | convolution fusion | flops 104857600 | bytes 2670592 | tf_op jit(solution)/shard_map/dot_general | solution.py:43
  106.9 0.4 fusion.8
  107.3 0.1 fusion.73
  107.4 0.2 convolution_add_fusion.4
  107.6 0.3 fusion.107
  107.9 0.2 multiply_reduce_fusion.2
  108.2 0.7 fusion.3
  109.0 0.3 copy-done.2
  109.3 0.4 fusion.9
  109.7 0.2 fusion.7
  109.9 0.2 fusion.26
  110.1 0.3 multiply_convert_fusion.1
  110.4 0.5 fusion.101
  111.0 0.1 add_convert_fusion.1
  111.1 0.2 fusion.10
  111.3 0.2 fusion.32
  111.5 0.3 multiply_convert_fusion
  111.8 0.1 fusion.50
  112.0 0.1 fusion.71
  112.1 0.1 fusion.59
  112.2 0.1 fusion.68
  112.4 0.1 fusion.66
  112.5 0.1 fusion.46
  112.6 0.2 fusion.44
  112.8 0.2 fusion.53
  113.0 0.1 fusion.63
  113.1 0.1 fusion.56
  113.3 0.2 fusion.38
  113.5 0.2 fusion.37
  113.7 0.5 fusion.100
  114.3 0.2 fusion.43
  114.5 0.1 fusion.108
  114.7 0.1 fusion.109
  114.9 0.1 fusion.110
  115.2 0.1 fusion.111
  115.4 0.1 fusion.112
  115.6 0.1 fusion.113
  115.8 0.1 fusion.114
  116.0 0.1 fusion.115
  116.3 32.2 %psum.7 = f32[1,8,256]{2,0,1:T(1,128)S(1)} all-reduce(f32[1,8,256]{2,0,1:T(1,128)S(1)} %constant_dynamic-update-slice_fusion), channel_id=1, replica_groups=mesh['query'=2,'corpus'=16] {'corpus'}, use_global_device_ids=true, to_apply=%region_9.10 | all-reduce | flops 2048 | bytes 16384 | tf_op jit(solution)/shard_map/psum | solution.py:186
  148.6 6.3 %all_to_all.12 = f32[1,8,256]{2,0,1:T(1,128)S(1)} all-to-all(f32[1,8,256]{2,0,1:T(1,128)S(1)} %psum.7), channel_id=1, replica_groups=mesh['query'=2,'corpus'=16] {'query'}, dimensions={1} | all-to-all | bytes 16384 | tf_op jit(solution)/shard_map/all_to_all | solution.py:187
  155.0 0.6 fusion.11
  155.6 4.3 %all_gather.19 = bf16[2,8,256]{2,0,1:T(2,128)(2,1)S(1)} all-gather(bf16[2,4,256]{2,0,1:T(2,128)(2,1)S(1)} %fusion.11), channel_id=1, replica_groups=mesh['query'=2,'corpus'=16] {'query'}, dimensions={1}, use_global_device_ids=true | all-gather | bytes 12288 | tf_op jit(solution)/shard_map/all_gather | solution.py:191
  160.0 1.0 convolution_multiply_fusion
  (79 shorter events, 1.4 us)
Async XLA Ops:
  6.5 148.5 %copy-start = (f32[4,256,256]{2,1,0:T(8,128)S(1)}, f32[4,256,256]{2,1,0:T(8,128)}, u32[]{:S(2)}) copy-start(f32[4,256,256]{2,1,0:T(8,128)} %param.29) | copy-start | bytes 3145732
  6.5 28.1 %copy-start.12 = (bf16[2,320,20]{1,0,2:T(2,128)(2,1)S(1)}, bf16[2,320,20]{1,0,2:T(2,128)(2,1)}, u32[]{:S(2)}) copy-start(bf16[2,320,20]{1,0,2:T(2,128)(2,1)} %param.22) | copy-start | bytes 76804
  6.5 55.6 %all-gather.5.cloned.1.call-start = ((), (), s32[]{:S(2)}) async-start(), calls=%async_computation.2 | async-start | bytes 1740800 | tf_op jit(solution)/shard_map/all_gather | solution.py:158
  7.3 97.1 %all-gather.3.cloned.1.call-start = ((), (), s32[]{:S(2)}) async-start(), calls=%async_computation.1 | async-start | bytes 4177920 | tf_op jit(solution)/shard_map/all_gather | solution.py:157
  54.3 3.4 %copy-start.16 = (f32[2,320]{1,0:T(2,128)S(1)}, f32[2,320]{1,0:T(2,128)}, u32[]{:S(2)}) copy-start(f32[2,320]{1,0:T(2,128)} %param.24) | copy-start | bytes 7684
  54.3 4.0 %copy-start.17 = (f32[2,320]{1,0:T(2,128)S(1)}, f32[2,320]{1,0:T(2,128)}, u32[]{:S(2)}) copy-start(f32[2,320]{1,0:T(2,128)} %param.23) | copy-start | bytes 7684
  54.3 4.0 %copy-start.21 = (s32[1,2]{1,0:T(1,128)S(1)}, s32[1,2]{1,0:T(1,128)}, u32[]{:S(2)}) copy-start(s32[1,2]{1,0:T(1,128)} %param.18) | copy-start | bytes 28
  54.3 4.3 %copy-start.6 = (bf16[1,2,32,320]{3,2,1,0:T(8,128)(2,1)S(1)}, bf16[1,2,32,320]{3,2,1,0:T(8,128)(2,1)}, u32[]{:S(2)}) copy-start(bf16[1,2,32,320]{3,2,1,0:T(8,128)(2,1)} %param.17) | copy-start | bytes 122884
  54.3 4.3 %copy-start.11 = (bf16[1,2,32,320]{3,2,1,0:T(8,128)(2,1)S(1)}, bf16[1,2,32,320]{3,2,1,0:T(8,128)(2,1)}, u32[]{:S(2)}) copy-start(bf16[1,2,32,320]{3,2,1,0:T(8,128)(2,1)} %param.16) | copy-start | bytes 122884
  59.6 8.3 %copy-start.14 = (f32[64]{0:T(128)}, f32[64]{0:T(128)S(1)}, u32[]{:S(2)}) copy-start(f32[64]{0:T(128)S(1)} %broadcast_multiply_fusion.5) | copy-start | bytes 772
  59.8 2.4 %copy-start.18 = (f32[64]{0:T(128)}, f32[64]{0:T(128)S(1)}, u32[]{:S(2)}) copy-start(f32[64]{0:T(128)S(1)} %add_rsqrt_fusion.1) | copy-start | bytes 772
  60.7 0.6 copy-start.4
  104.3 2.9 %copy-start.10 = (bf16[2,3,320,16]{2,3,1,0:T(8,128)(2,1)S(1)}, bf16[2,3,320,16]{2,3,1,0:T(8,128)(2,1)}, u32[]{:S(2)}) copy-start(bf16[2,3,320,16]{2,3,1,0:T(8,128)(2,1)} %param.25) | copy-start | bytes 184324
  104.3 3.1 %copy-start.5 = (f32[1,2,32,320]{3,2,1,0:T(8,128)S(1)}, f32[1,2,32,320]{3,2,1,0:T(8,128)}, u32[]{:S(2)}) copy-start(f32[1,2,32,320]{3,2,1,0:T(8,128)} %get-tuple-element.14) | copy-start | bytes 245764
  104.3 3.9 %copy-start.1 = (bf16[2,320,2560]{1,2,0:T(8,128)(2,1)S(1)}, bf16[2,320,2560]{1,2,0:T(8,128)(2,1)}, u32[]{:S(2)}) copy-start(bf16[2,320,2560]{1,2,0:T(8,128)(2,1)} %all-gather.3.cloned.1.call-done) | copy-start | bytes 9830404
  106.8 1.3 copy-start.13
  107.9 1.4 copy-start.2
  108.2 1.5 copy-start.7
  110.9 0.9 copy-start.9
  110.9 1.6 copy-start.8
  111.3 2.0 %copy-start.22 = (bf16[2,2560,16]{1,2,0:T(8,128)(2,1)S(1)}, bf16[2,2560,16]{1,2,0:T(8,128)(2,1)}, u32[]{:S(2)}) copy-start(bf16[2,2560,16]{1,2,0:T(8,128)(2,1)} %param.28) | copy-start | bytes 491524
  111.5 2.2 %copy-start.15 = (f32[64]{0:T(128)S(1)}, f32[64]{0:T(128)}, u32[]{:S(2)}) copy-start(f32[64]{0:T(128)} %copy-done.14) | copy-start | bytes 772
  111.5 2.2 %copy-start.19 = (f32[64]{0:T(128)S(1)}, f32[64]{0:T(128)}, u32[]{:S(2)}) copy-start(f32[64]{0:T(128)} %copy-done.18) | copy-start | bytes 772
  113.7 46.3 %copy-start.3 = (bf16[256,2048]{1,0:T(8,128)(2,1)S(1)}, bf16[256,2048]{1,0:T(8,128)(2,1)}, u32[]{:S(2)}) copy-start(bf16[256,2048]{1,0:T(8,128)(2,1)} %param.30) | copy-start | bytes 3145732
  113.7 46.3 %copy-start.20 = (f32[256]{0:T(256)S(1)}, f32[256]{0:T(256)}, u32[]{:S(2)}) copy-start(f32[256]{0:T(256)} %param.31) | copy-start | bytes 3076
Sparse Core Ops, SparseCore 0:
  9.5 43.8 all-gather.4
  55.7 48.5 all-gather.2

commit v2 on v1

--- a/solution.py
+++ b/solution.py
@@ -3,6 +3,8 @@
 import jax
 import jax.numpy as jnp
 from jax import lax
+from jax.experimental import pallas as pl
+from jax.experimental.pallas import tpu as pltpu
 from jax.sharding import PartitionSpec as P
 
 plan_len = 1000
@@ -196,6 +198,419 @@
     return raw * store_scale[None, :]
 
 
+MESH = pl.DeviceIdType.MESH
+f32 = jnp.float32
+bf16 = jnp.bfloat16
+zs_n, ys_n, cores, ranks = 4, 2, 2, 16
+small = 128
+wide = 160
+slot = small + wide
+half = slot // 2
+lanes = 384
+strips = 4
+
+
+def dot(a, b, dims=((1,), (0,)), precision=None):
+    return lax.dot_general(a, b, (dims, ((), ())), preferred_element_type=f32, precision=precision)
+
+
+def dot_t(a, b):
+    return dot(a, b, ((1,), (1,)))
+
+
+def one_hot(shape, fn):
+    r = lax.broadcasted_iota(jnp.int32, shape, 0)
+    c = lax.broadcasted_iota(jnp.int32, shape, 1)
+    return fn(r, c).astype(f32).astype(bf16)
+
+
+def kernel(
+    steps_ref, clean_ref, noise_ref, win_ref, wfi_ref, wfo_ref, wout_ref, gain_ref, bias_ref,
+    cin_ref, fin_ref, cout_ref, fout_ref, precond_hbm, store_hbm, raw_ref,
+    w, d, dfo, clean_p, noise_p, gain_p, bias_p, ecin, efin, ecout, efout, xin_s, xhat_s, isig_s, norm_s, gel_s, der_s, mix_s, xout_s,
+    part, box, pre, precond, store,
+    send, recv, all_send, all_recv, pre_send, pre_recv, local,
+):
+    x = lax.axis_index("query")
+    me = lax.axis_index("corpus")
+    z = me // (ys_n * cores)
+    y = (me // cores) % ys_n
+    k = me % cores
+    flat = x * ranks + me
+    devices = 2 * ranks
+    share = win_ref.shape[2]
+
+    barrier = pltpu.get_barrier_semaphore()
+
+    @pl.loop(0, devices)
+    def _(i):
+        @pl.when(i != flat)
+        def _():
+            pl.semaphore_signal(barrier, inc=1, device_id=(i // ranks, i % ranks), device_id_type=MESH)
+
+    fetch_p = pltpu.make_async_copy(precond_hbm, precond, local.at[0])
+    fetch_s = pltpu.make_async_copy(store_hbm, store, local.at[1])
+    fetch_p.start()
+    fetch_s.start()
+
+    places = [
+        one_hot((small, share), lambda r, c, s=s: r == share * s + c) for s in range(2 + strips)
+    ]
+    same = one_hot((wide, wide), lambda r, c: r == c)
+    channels, hidden = win_ref.shape[1], fin_ref.shape[1]
+
+    def tall(v):
+        if v.shape[0] == lanes:
+            return v
+        return jnp.concatenate([v, jnp.zeros((lanes - v.shape[0], v.shape[1]), v.dtype)], axis=0)
+
+    for b in range(2):
+        rows = dot_t(places[0], tall(win_ref[b])) + dot_t(places[1], tall(wout_ref[b]))
+        for s in range(strips):
+            rows += dot_t(places[2 + s], tall(wfo_ref[b, lanes * s : min(lanes * (s + 1), hidden), :]))
+        w[b, me, 0:small, :] = rows.astype(bf16)
+        w[b, me, small:slot, :] = dot_t(same, tall(wfi_ref[b])).astype(bf16)
+
+    pl.semaphore_wait(barrier, devices - 1)
+
+    def src_of(zs, yy):
+        return (zs * ys_n + yy) * cores + k
+
+    def unit(b, src, p):
+        return w.at[b, src, pl.ds(pl.multiple_of(p * half, 16), half)]
+
+    def copy(kind, b, src, p, qd, cd):
+        return pltpu.make_async_remote_copy(
+            src_ref=unit(b, src, p), dst_ref=unit(b, src, p),
+            send_sem=send.at[kind, b, src, p], recv_sem=recv.at[b, src, p],
+            device_id=(qd, cd), device_id_type=MESH,
+        )
+
+    started = []
+
+    def start(guard, *what):
+        started.append((guard, what))
+        if guard is None:
+            copy(*what).start()
+        else:
+            @pl.when(guard)
+            def _():
+                copy(*what).start()
+
+    def arrive(guard, b, src, p):
+        def go():
+            copy(0, b, src, p, x, me ^ 1).wait_recv()
+        if guard is None:
+            go()
+        else:
+            pl.when(guard)(go)
+
+    up, down = me + ys_n * cores, me - ys_n * cores
+    beside, twin = me + cores * (1 - 2 * y), me + 1 - 2 * k
+    far = 1 - x
+
+    def both(guard, more):
+        return more if guard is None else jnp.logical_and(guard, more)
+
+    def direct(b, dist):
+        sides = [(0, 0)] if dist == 0 else [(-1, 1), (1, 1)]
+        for side, _ in sides:
+            zs = z + side * dist
+            ok = None if dist == 0 else jnp.logical_and(zs >= 0, zs < zs_n)
+            src = src_of(zs, y)
+            for p in range(2):
+                if dist:
+                    arrive(ok, b, src, p)
+                if side <= 0:
+                    start(both(ok, z < zs_n - 1), 0, b, src, p, x, up)
+                if side >= 0:
+                    start(both(ok, z > 0), 1, b, src, p, x, down)
+                start(ok, 3, b, src, p, x, twin)
+            start(ok, 2, b, src, x, x, beside)
+
+    def cross(b, dist, relayed):
+        for side in ([0] if dist == 0 else [-1, 1]):
+            zs = z + side * dist
+            ok = None if dist == 0 else jnp.logical_and(zs >= 0, zs < zs_n)
+            src = src_of(zs, 1 - y)
+            if relayed:
+                arrive(ok, b, src, 1 - x)
+                start(ok, 3, b, src, 1 - x, x, twin)
+            else:
+                arrive(ok, b, src, x)
+                start(ok, 2, b, src, x, far, me)
+                start(ok, 3, b, src, x, x, twin)
+
+    def block_steps(b):
+        return [
+            lambda: direct(b, 0),
+            lambda: direct(b, 1),
+            lambda: (cross(b, 0, False), direct(b, 2)),
+            lambda: (cross(b, 1, False), direct(b, 3), cross(b, 0, True)),
+            lambda: (cross(b, 2, False), cross(b, 1, True)),
+            lambda: (cross(b, 3, False), cross(b, 2, True)),
+            lambda: cross(b, 3, True),
+        ]
+
+    def twins(b):
+        for i in range(zs_n * ys_n):
+            for p in range(2):
+                arrive(None, b, i * cores + (1 - k), p)
+
+    ki = cin_ref.shape[-1]
+    spread_in = one_hot((ki * ki, ki), lambda r, c: c == r // ki)
+    spread_out = one_hot((ki * ki, ki), lambda r, c: c == r % ki)
+
+    def spread_c(b):
+        for j in range(3):
+            ecin[b, j] = dot_t(spread_in, tall(cin_ref[b, j])).astype(bf16)
+            ecout[b, j] = dot_t(spread_out, tall(cout_ref[b, j])).astype(bf16)
+
+    def spread_f(b):
+        efin[b] = dot_t(spread_in, fin_ref[b]).astype(bf16)
+        for s in range(2):
+            cut = slice(hidden * s, hidden * (s + 1))
+            efout[b, s] = dot_t(spread_out, fout_ref[b, cut]).astype(bf16)
+
+    def widen():
+        for wide_ref, narrow in ((clean_p, clean_ref), (noise_p, noise_ref), (gain_p, gain_ref), (bias_p, bias_ref)):
+            wide_ref[...] = jnp.zeros_like(wide_ref)
+            wide_ref[:, 0:channels] = narrow[...]
+        for b in range(2):
+            for j in range(2):
+                d[b, j, channels:lanes, :] = jnp.zeros((lanes - channels, lanes), bf16)
+            dfo[b, channels:lanes, :] = jnp.zeros((lanes - channels, hidden), bf16)
+
+    group = 4
+    outs = group * share
+    many = 2 + strips
+
+    def unpack(b):
+        pick = jnp.concatenate(
+            [
+                one_hot(
+                    (outs, group * small),
+                    lambda r, c, s=s: c == (r // share) * small + share * s + r % share,
+                )
+                for s in range(many)
+            ],
+            axis=0,
+        )
+        for g in range(ranks // group):
+            got = dot(pick, w[b, group * g : group * (g + 1), 0:small, :].reshape(group * small, lanes)).astype(bf16)
+            for s in range(2):
+                d[b, s, outs * g : outs * (g + 1), :] = got[outs * s : outs * (s + 1)]
+            for s in range(strips):
+                end = min(lanes * (s + 1), hidden)
+                dfo[b, outs * g : outs * (g + 1), lanes * s : end] = got[
+                    outs * (2 + s) : outs * (3 + s), 0 : end - lanes * s
+                ]
+
+    def ffin(b, s):
+        return w[b, ranks // 2 * s : ranks // 2 * (s + 1), small:slot, :].reshape(hidden, lanes)
+
+    rows_each = clean_ref.shape[0] // 2
+    rows = 2 * rows_each
+    live = lax.broadcasted_iota(jnp.int32, (1, lanes), 1) < channels
+
+    def mean(v):
+        return jnp.sum(v, axis=-1, keepdims=True) * (1.0 / channels)
+
+    def levels():
+        order = (
+            lax.broadcasted_iota(jnp.int32, (8, 128), 0) * 128 + lax.broadcasted_iota(jnp.int32, (8, 128), 1)
+        )
+        rooted = math.sqrt(0.00085) + (math.sqrt(0.012) - math.sqrt(0.00085)) * order.astype(f32) / (plan_len - 1)
+        terms = jnp.log1p(-rooted * rooted)
+        first = lax.broadcasted_iota(jnp.int32, (rows, 1), 0) < rows_each
+        total = [
+            jnp.sum(jnp.where(order <= steps_ref[t], terms, 0.0), axis=(0, 1), keepdims=True) for t in range(2)
+        ]
+        kept = jnp.exp(jnp.where(first, total[0], total[1]))
+        return jnp.sqrt(kept), jnp.sqrt(1.0 - kept)
+
+    def forward(b, stream):
+        xin = stream.astype(bf16)
+        xin_s[b] = xin
+        inner = dot_t(xin, d[b, 0])
+        centred = jnp.where(live, inner - mean(inner), 0.0)
+        inv = lax.rsqrt(mean(centred * centred) + 1e-05)
+        xhat = centred * inv
+        xhat_s[b] = xhat
+        isig_s[b] = inv
+        normed = (xhat * gain_p[b : b + 1] + bias_p[b : b + 1]).astype(bf16)
+        norm_s[b] = normed
+        value = dot_t(normed, ffin(b, 0))
+        gate = dot_t(normed, ffin(b, 1))
+        cumul = 0.5 * (1.0 + lax.erf(gate * (1.0 / math.sqrt(2.0))))
+        density = jnp.exp(-0.5 * gate * gate) * (1.0 / math.sqrt(2.0 * math.pi))
+        gel = gate * cumul
+        gel_s[b] = gel
+        der_s[b] = value * (cumul + gate * density)
+        mixed = (value * gel).astype(bf16)
+        mix_s[b] = mixed
+        inner += dot_t(mixed, dfo[b])
+        xout = inner.astype(bf16)
+        xout_s[b] = xout
+        return stream + dot_t(xout, d[b, 1])
+
+    def record(layer, left, right):
+        part[layer // 4, layer % 4 : layer % 4 + 1, :] = jnp.sum(left * right, axis=0, keepdims=True)
+
+    def backward(b, ds):
+        dout = ds.astype(bf16)
+        d2 = dot(dout, d[b, 1])
+        d2b = d2.astype(bf16)
+        dmix = dot(d2b, dfo[b])
+        dval = (dmix * gel_s[b]).astype(bf16)
+        dgate = (dmix * der_s[b]).astype(bf16)
+        dnorm = dot(dval, ffin(b, 0)) + dot(dgate, ffin(b, 1))
+        right = dot_t(dval, efout[b, 0]) + dot_t(dgate, efout[b, 1])
+        left = dot_t(mix_s[b], efin[b])
+        g = dnorm * gain_p[b : b + 1]
+        xhat = xhat_s[b]
+        dinner = jnp.where(live, d2 + isig_s[b] * (g - mean(g) - xhat * mean(g * xhat)), 0.0)
+        dinb = dinner.astype(bf16)
+        record(4 * b + 1, dot_t(norm_s[b], ecin[b, 1]), right)
+        record(4 * b + 2, left, dot_t(d2b, ecout[b, 1]))
+        record(4 * b + 3, dot_t(xout_s[b], ecin[b, 2]), dot_t(dout, ecout[b, 2]))
+        record(4 * b, dot_t(xin_s[b], ecin[b, 0]), dot_t(dinb, ecout[b, 0]))
+        return ds + dot(dinb, d[b, 0]) if b else None
+
+    first, second = block_steps(0), block_steps(1)
+    lag = 2
+    fill = [widen, lambda: spread_c(0), lambda: spread_c(1), lambda: spread_f(0), lambda: spread_f(1)]
+    for i in range(len(first) + lag):
+        if i < len(first):
+            first[i]()
+        if 0 <= i - lag < len(second):
+            second[i - lag]()
+        if i < len(fill):
+            fill[i]()
+    twins(0)
+    unpack(0)
+    signal, spread = levels()
+    noise = noise_p[...].astype(f32)
+    stream = signal * clean_p[...].astype(f32) + spread * noise
+    stream = forward(0, stream)
+    twins(1)
+    unpack(1)
+    stream = forward(1, stream)
+    ds = (stream - noise) * (1.0 / math.sqrt(2 * rows_each * ranks))
+    ds = backward(1, ds)
+    backward(0, ds)
+
+    box[flat] = part[x]
+
+    def give(i):
+        return pltpu.make_async_remote_copy(
+            src_ref=part.at[i // ranks], dst_ref=box.at[flat], send_sem=all_send.at[0], recv_sem=all_recv.at[0],
+            device_id=(i // ranks, i % ranks), device_id_type=MESH,
+        )
+
+    @pl.loop(0, devices)
+    def _(i):
+        @pl.when(i != flat)
+        def _():
+            give(i).start()
+
+    fetch_p.wait()
+    fetch_s.wait()
+    rest = box.at[pl.ds(0, devices - 1)]
+    pltpu.make_async_copy(rest, rest, all_recv.at[0]).wait()
+    grads = jnp.concatenate(
+        [jnp.sum(box[0:ranks], axis=0), jnp.sum(box[ranks:devices], axis=0)], axis=0
+    )
+    where_row = lax.broadcasted_iota(jnp.int32, (8, 1), 0) % 4
+    own = jnp.zeros_like(grads)
+    for l in range(4):
+        own = jnp.where(where_row == l, dot(grads, precond[l], precision=lax.Precision.HIGHEST), own)
+    pre[x] = jnp.concatenate([own, jnp.zeros_like(own)], axis=0).astype(bf16)
+    swap = pltpu.make_async_remote_copy(
+        src_ref=pre.at[x], dst_ref=pre.at[x], send_sem=pre_send.at[0], recv_sem=pre_recv.at[0],
+        device_id=(far, me), device_id_type=MESH,
+    )
+    swap.start()
+    swap.wait()
+    low = jnp.zeros((1, raw_ref.shape[1]), f32)
+    high = jnp.zeros((1, raw_ref.shape[1]), f32)
+    for h in range(2):
+        for l in range(4):
+            at = 4 * h + l
+            r = dot_t(pre[h], store[:, 256 * at : 256 * (at + 1)])
+            low += r[l : l + 1]
+            high += r[4 + l : 5 + l]
+    raw_ref[...] = jnp.concatenate([low, high], axis=0)
+
+    pltpu.make_async_copy(rest, rest, all_send.at[0]).wait()
+    for guard, what in started:
+        def done(what=what):
+            copy(*what).wait_send()
+        if guard is None:
+            done()
+        else:
+            pl.when(guard)(done)
+
+
+def fused(
+    clean_feats, noise_draw, timesteps, weight_in, weight_ffin, weight_ffout, weight_out, norm_gain, norm_bias,
+    sketch_cin, sketch_fin, sketch_cout, sketch_fout, precond, store_grads, store_scale,
+):
+    channels = clean_feats.shape[-1]
+    rows = clean_feats.shape[1] * clean_feats.shape[2]
+    hidden = sketch_fin.shape[1]
+    width = sketch_cin.shape[-1] ** 2
+    vmem = pl.BlockSpec(memory_space=pltpu.VMEM)
+    anywhere = pl.BlockSpec(memory_space=pl.ANY)
+    raw = pl.pallas_call(
+        kernel,
+        out_shape=jax.ShapeDtypeStruct((2, store_grads.shape[0]), f32),
+        in_specs=[pl.BlockSpec(memory_space=pltpu.SMEM)] + [vmem] * 12 + [anywhere] * 2,
+        out_specs=vmem,
+        scratch_shapes=[
+            pltpu.VMEM((2, ranks, slot, lanes), bf16),
+            pltpu.VMEM((2, 2, lanes, lanes), bf16),
+            pltpu.VMEM((2, lanes, hidden), bf16),
+            pltpu.VMEM((rows, lanes), bf16),
+            pltpu.VMEM((rows, lanes), bf16),
+            pltpu.VMEM((2, lanes), f32),
+            pltpu.VMEM((2, lanes), f32),
+            pltpu.VMEM((2, 3, width, lanes), bf16),
+            pltpu.VMEM((2, width, hidden), bf16),
+            pltpu.VMEM((2, 3, width, lanes), bf16),
+            pltpu.VMEM((2, 2, width, hidden), bf16),
+            pltpu.VMEM((2, rows, lanes), bf16),
+            pltpu.VMEM((2, rows, lanes), f32),
+            pltpu.VMEM((2, rows, 1), f32),
+            pltpu.VMEM((2, rows, lanes), bf16),
+            pltpu.VMEM((2, rows, hidden), f32),
+            pltpu.VMEM((2, rows, hidden), f32),
+            pltpu.VMEM((2, rows, hidden), bf16),
+            pltpu.VMEM((2, rows, lanes), bf16),
+            pltpu.VMEM((2, 4, width), f32),
+            pltpu.VMEM((2 * ranks, 4, width), f32),
+            pltpu.VMEM((2, 16, width), bf16),
+            pltpu.VMEM(precond.shape, f32),
+            pltpu.VMEM(store_grads.shape, bf16),
+            pltpu.SemaphoreType.DMA((4, 2, ranks, 2)),
+            pltpu.SemaphoreType.DMA((2, ranks, 2)),
+            pltpu.SemaphoreType.DMA((1,)),
+            pltpu.SemaphoreType.DMA((1,)),
+            pltpu.SemaphoreType.DMA((1,)),
+            pltpu.SemaphoreType.DMA((1,)),
+            pltpu.SemaphoreType.DMA((2,)),
+        ],
+        compiler_params=pltpu.CompilerParams(
+            collective_id=0, has_side_effects=True, vmem_limit_bytes=60 * 1024 * 1024
+        ),
+    )(
+        timesteps.reshape(-1), clean_feats.reshape(rows, channels), noise_draw.reshape(rows, channels),
+        weight_in, weight_ffin, weight_ffout, weight_out, norm_gain, norm_bias,
+        sketch_cin, sketch_fin, sketch_cout, sketch_fout, precond, store_grads,
+    )
+    return raw * store_scale[None, :]
+
+
 def solution(mesh):
     placed = (
         P("query", None, "corpus", None),
@@ -215,8 +630,9 @@
         P(("query", "corpus"), None),
         P(("query", "corpus")),
     )
+    planned = mesh.shape["query"] == 2 and mesh.shape["corpus"] == ranks
     return jax.shard_map(
-        on_device,
+        fused if planned else on_device,
         mesh=mesh,
         in_specs=placed,
         out_specs=P(None, ("query", "corpus")),

time: 168 us -> 81.1 us (0.48)
  blocking collectives: 87.6 us -> 0 us
  Pallas kernels: 0 us -> 67.9 us
  waiting for transfers between devices: 37.9 us -> 0 us
  between operations: 13.9 us -> 0.03 us
  matrix products: 13.5 us -> 0 us
    pallas_call x0 -> x1, Pallas kernels: none -> 67.9 us  [fused(): pl.pallas_call(kernel, out_shape=jax.ShapeDtypeStruct((2, store_grads.sha...]
    all_gather x3 -> x0, blocking collectives: 49 us -> none  [the longest x1 25 us: on_device(): lax.all_gather(weight_in, 'corpus', axis=2, tiled=True)]
    all_gather x2 -> x0, waiting for transfers between devices: 36.5 us -> none  [the longest x1 36.5 us: on_device(): lax.all_gather(weight_ffin, 'corpus', axis=2, tiled=True)]
    psum x1 -> x0, blocking collectives: 32.2 us -> none  [on_device(): totals = lax.psum(partial_grads, 'corpus')]
    dot_general x41 -> x0, matrix products: 13.5 us -> none  [the longest x2 3.18 us: block_forward(): jnp.dot(normalized_input, weight_ffin, preferred_element_type=jnp.float32)]
    slice x5 -> x0, local copies, waits for them, and re-layouts: 7.66 us -> none  [the longest x3 7.04 us: fetch_forward(): return tuple((member[block] for member in gathered))]
    unnamed x57 -> x18, local copies, waits for them, and re-layouts: 4.61 us -> 11.7 us
    all_to_all x1 -> x0, blocking collectives: 6.35 us -> none  [on_device(): lax.all_to_all(totals, 'query', split_axis=1, concat_axis=0, tiled=True)]
  transfers between devices with their start and end apart: 2 -> 0, of which waited for: 1 -> 0; matrix products, arithmetic and copies ran while one was open for 9% -> 0% of each run, Pallas kernels for 0% -> 0%
where the time goes in v2:
time: 81.1 us; the launch traced here: 80.9 us
  Pallas kernels  67.9 us (84%)
  local copies, waits for them, and re-layouts  11.7 us (14%)
  other arithmetic  1.24 us (2%)
    pallas_call x1, Pallas kernels, fused(): pl.pallas_call(kernel, out_shape=jax.ShapeDtypeStruct((2, store_grads.sha...  67.9 us
    unnamed x18, local copies, waits for them, and re-layouts  11.7 us

profile of v2, /device:TPU:0, one launch (start us, length us, event | category | flops | bytes accessed | tf_op | source)
XLA Modules:
  0.0 80.9 jit_solution(7080247338134407196)
XLA Ops:
  0.0 0.0 copy-start.3
  0.0 0.0 copy-start.1
  0.0 1.6 %copy.17.win_ref = bf16[2,320,20]{2,1,0:T(8,128)(2,1)} copy(bf16[2,320,20]{1,0,2:T(2,128)(2,1)} %param.19) | data formatting | bytes 51200 | tf_op args[3]
  1.6 0.0 copy-start.2
  1.6 1.6 %copy.20.wout_ref = bf16[2,320,20]{2,1,0:T(8,128)(2,1)} copy(bf16[2,320,20]{1,0,2:T(2,128)(2,1)} %param.22) | data formatting | bytes 51200 | tf_op args[6]
  3.3 1.8 %copy.18.wfi_ref = bf16[2,320,160]{2,1,0:T(8,128)(2,1)} copy(bf16[2,320,160]{1,2,0:T(8,128)(2,1)} %param.20) | data formatting | bytes 409600 | tf_op args[4]
  5.1 0.0 copy-start
  5.1 1.9 %copy.21.cin_ref = bf16[2,3,320,16]{3,2,1,0:T(8,128)(2,1)} copy(bf16[2,3,320,16]{2,3,1,0:T(8,128)(2,1)} %param.25) | data formatting | bytes 122880 | tf_op args[9]
  7.0 0.0 copy-done.3
  7.0 1.0 %copy.23.cout_ref = bf16[2,3,320,16]{3,2,1,0:T(8,128)(2,1)} copy(bf16[2,3,320,16]{2,3,1,0:T(8,128)(2,1)S(1)} %copy-done.3) | data formatting | bytes 122880 | tf_op args[11]
  8.0 0.0 copy-done.1
  8.0 1.2 %copy.19.wfo_ref = bf16[2,1280,20]{2,1,0:T(8,128)(2,1)} copy(bf16[2,1280,20]{1,0,2:T(2,128)(2,1)S(1)} %copy-done.1) | data formatting | bytes 204800 | tf_op args[5]
  9.2 0.0 copy-done.2
  9.2 1.1 %copy.22.fin_ref = bf16[2,1280,16]{2,1,0:T(8,128)(2,1)} copy(bf16[2,1280,16]{1,2,0:T(8,128)(2,1)S(1)} %copy-done.2) | data formatting | bytes 163840 | tf_op args[10]
  10.3 0.0 copy-done
  10.3 1.5 %copy.24.fout_ref = bf16[2,2560,16]{2,1,0:T(8,128)(2,1)} copy(bf16[2,2560,16]{1,2,0:T(8,128)(2,1)S(1)} %copy-done) | data formatting | bytes 327680 | tf_op args[12]
  11.7 0.0 copy-start.4
  11.7 67.9 %shard_map.154 = f32[2,256]{1,0:T(2,128)} custom-call(s32[2]{0:T(128)} %bitcast.5, bf16[64,320]{1,0:T(8,128)(2,1)} %bitcast.3, bf16[64,320]{1,0:T(8,128)(2,1)} %bitcast.4, bf16[2,320,20]{2,1,0:T(8,128)(2,1)} %copy.17.win_ref, bf16[2,320,160]{2,1,0:T(8,128)(2,1)} %copy.18.wfi_ref, bf16[2,1280,20]{2,1,0:T(8,128)(2,1)} %copy.19.wfo_ref, ...), custom_call_target="tpu_custom_call" | custom-call | tf_op jit(solution)/shard_map/pallas_call | solution.py:565
  79.6 0.0 copy-done.4
  79.6 1.2 %broadcast_multiply_fusion = f32[2,256]{1,0:T(2,128)} fusion(f32[2,256]{1,0:T(2,128)} %shard_map.154, f32[256]{0:T(256)S(1)} %copy-done.4), kind=kLoop, calls=%fused_computation | loop fusion | flops 512 | bytes 5120 | tf_op jit(solution)/shard_map/mul | solution.py:611
Async XLA Ops:
  0.0 7.0 %copy-start.3 = (bf16[2,3,320,16]{2,3,1,0:T(8,128)(2,1)S(1)}, bf16[2,3,320,16]{2,3,1,0:T(8,128)(2,1)}, u32[]{:S(2)}) copy-start(bf16[2,3,320,16]{2,3,1,0:T(8,128)(2,1)} %param.27) | copy-start | bytes 184324
  0.0 8.0 %copy-start.1 = (bf16[2,1280,20]{1,0,2:T(2,128)(2,1)S(1)}, bf16[2,1280,20]{1,0,2:T(2,128)(2,1)}, u32[]{:S(2)}) copy-start(bf16[2,1280,20]{1,0,2:T(2,128)(2,1)} %param.21) | copy-start | bytes 307204
  1.6 7.5 %copy-start.2 = (bf16[2,1280,16]{1,2,0:T(8,128)(2,1)S(1)}, bf16[2,1280,16]{1,2,0:T(8,128)(2,1)}, u32[]{:S(2)}) copy-start(bf16[2,1280,16]{1,2,0:T(8,128)(2,1)} %param.26) | copy-start | bytes 245764
  5.1 5.2 %copy-start = (bf16[2,2560,16]{1,2,0:T(8,128)(2,1)S(1)}, bf16[2,2560,16]{1,2,0:T(8,128)(2,1)}, u32[]{:S(2)}) copy-start(bf16[2,2560,16]{1,2,0:T(8,128)(2,1)} %param.28) | copy-start | bytes 491524
  11.7 67.9 %copy-start.4 = (f32[256]{0:T(256)S(1)}, f32[256]{0:T(256)}, u32[]{:S(2)}) copy-start(f32[256]{0:T(256)} %param.31) | copy-start | bytes 3076
